TPU v7x, 512 devices: a whole 4x4x16 slice. The times are simulated.
512 devices in a mesh: dp: 32 (over z, y_hi), node: 16 (over y_lo, x, core).
Axes of the slice: x: 4, y: 4 (y_hi: 2, y_lo: 2; y = y_hi * 2 + y_lo), z: 16, core: 2. Of those that a mesh axis runs over, the one named last changes fastest.
Arguments:
- tokens_in: bfloat16 [32768, 4096], P('dp', 'node'), may hold values from -6 to 6
- out_grads: bfloat16 [32768, 4096], P('dp'), may hold values from -0.0078125 to 0.0078125
- left_old: float32 [4096, 4096], P('node', 'dp'), may hold values from -0.1 to 4.1, as said below
- right_old: float32 [4096, 4096], P('node', 'dp'), may hold values from -0.1 to 4.1, as said below
Outputs:
- left_out: float32 [4096, 4096], P('node', 'dp')
- right_out: float32 [4096, 4096], P('node', 'dp')
Inputs may be any that keep to these rules, and one draw needn't show every extreme that they name: `left_old`: symmetric. `right_old`: symmetric.
All inputs are finite; a program needn't handle non-finite values.
Results may differ from a plain program's by a relative error of at most 0.0021.
Values may be sent and summed in bfloat16 or wider, within the bound.
A program may use at most 64 MiB of HBM per device.

v0:
```python
import jax
import jax.numpy as jnp
from jax import lax
from jax.sharding import PartitionSpec as P

ema_decay = 0.95


def from_root(value, axis, source):
    kept = jnp.where(lax.axis_index(axis) == source, value, 0).astype(value.dtype)
    return lax.psum(kept, axis)


def contract_first(left, right):
    return lax.dot_general(
        left, right, (((0,), (0,)), ((), ())), preferred_element_type=jnp.float32
    )


def contract_last(left, right):
    return lax.dot_general(
        left, right, (((1,), (1,)), ((), ())), preferred_element_type=jnp.float32
    )


def shards(tokens_in, out_grads, left_old, right_old):
    group_ratio = lax.axis_size("dp") // lax.axis_size("node")
    dp_index = lax.axis_index("dp")
    slab_width = left_old.shape[1]
    summed = lax.psum(contract_first(out_grads, tokens_in), "dp")
    row_panel = summed.astype(jnp.bfloat16)
    own_tile = lax.dynamic_slice_in_dim(row_panel, dp_index * slab_width, slab_width, 0)
    crossed = lax.all_to_all(row_panel, "node", split_axis=0, concat_axis=1, tiled=True)
    right_new = contract_last(crossed, lax.all_gather(own_tile, "node", axis=1, tiled=True))
    local_rows = lax.dynamic_slice_in_dim(
        row_panel, dp_index % group_ratio * slab_width, slab_width, 1
    )
    row_slab = from_root(local_rows, "node", dp_index // group_ratio)
    left_new = contract_first(row_panel, row_slab)
    left_out = ema_decay * left_old + (1.0 - ema_decay) * left_new
    right_out = ema_decay * right_old + (1.0 - ema_decay) * right_new
    return (left_out, right_out)


def solution(mesh):
    placed = (P("dp", "node"), P("dp", None), P("node", "dp"), P("node", "dp"))
    return jax.shard_map(
        shards,
        mesh=mesh,
        in_specs=placed,
        out_specs=(P("node", "dp"), P("node", "dp")),
        check_vma=False,
    )
```

profile of v0, /device:TPU:1, one launch (start us, length us, event | category | flops | bytes accessed | tf_op | source)
XLA Modules:
  0.0 433.9 jit_solution(7988224578985698390)
XLA Ops:
  7.2 0.0 copy-start
  7.2 0.0 all-reduce.3.cloned.1.call-start
  7.2 1.0 copy-done
  8.2 7.8 %fusion.2 = f32[4096,256]{1,0:T(8,128)} fusion(bf16[1024,4096]{1,0:T(8,128)(2,1)} %param.5, bf16[1024,256]{1,0:T(8,128)(2,1)S(1)} %copy-done), kind=kOutput, calls=%fused_computation.6 | convolution fusion | flops 2147483648 | bytes 13107200 | tf_op jit(solution)/shard_map/dot_general | solution.py:15
  16.0 202.3 %all-reduce.4 = bf16[4096,256]{1,0:T(8,128)(2,1)S(1)} all-reduce(f32[4096,256]{1,0:T(8,128)} %fusion.2), channel_id=1, replica_groups=mesh['dp'=32,'node'=16] {'dp'}, use_global_device_ids=true, to_apply=%region_0.0 | all-reduce | flops 1048576 | bytes 6291456 | tf_op jit(solution)/shard_map/psum | solution.py:30
  218.3 1.2 dynamic-slice_select_fusion
  219.5 0.0 all-reduce.3.cloned.1.call-update
  219.5 0.0 all-gather.2.cloned.1.call-start
  219.6 0.6 constant_dynamic-slice_fusion
  220.2 0.1 all-gather.2.cloned.1.call-update
  220.3 2.4 copy.6
  222.7 0.0 copy-start.1
  222.7 26.5 %all-to-all-start = ((bf16[16,256,256]{1,2,0:T(8,128)(2,1)}), bf16[16,256,256]{1,2,0:T(8,128)(2,1)}, u32[]{:S(2)}, u32[]{:S(2)}) async-start(bf16[16,256,256]{1,2,0:T(8,128)(2,1)} %copy.6), calls=%async_computation | async-start | bytes 4194304 | tf_op jit(solution)/shard_map/all_to_all | solution.py:33
  249.1 0.0 copy-start.2
  249.1 128.5 %all-reduce.3.cloned.1.call-done = bf16[4096,128]{1,0:T(8,128)(2,1)} async-done(((bf16[4096,128]{1,0:T(8,128)(2,1)}), bf16[4096,128]{1,0:T(8,128)(2,1)}) %all-reduce.3.cloned.1.call-update) | async-done | bytes 1048592 | tf_op jit(solution)/shard_map/psum | solution.py:11
  377.6 0.0 copy-done.1
  377.6 2.6 fusion.1
  380.2 43.6 %all-gather.2.cloned.1.call-done = bf16[128,4096]{1,0:T(8,128)(2,1)} async-done(((bf16[128,256]{1,0:T(8,128)(2,1)}), bf16[128,4096]{1,0:T(8,128)(2,1)}) %all-gather.2.cloned.1.call-update) | async-done | bytes 1048592 | tf_op jit(solution)/shard_map/all_gather | solution.py:34
  423.8 0.0 all-to-all-done
  423.8 0.0 copy-done.2
  423.8 3.3 fusion
Async XLA Ops:
  7.2 1.0 copy-start
  7.2 370.4 %all-reduce.3.cloned.1.call-start = ((), (), s32[]{:S(2)}) async-start(), calls=%async_computation.1 | async-start | bytes 2097152 | tf_op jit(solution)/shard_map/psum | solution.py:11
  219.5 204.3 %all-gather.2.cloned.1.call-start = ((), (), s32[]{:S(2)}) async-start(), calls=%async_computation.2 | async-start | bytes 1114112 | tf_op jit(solution)/shard_map/all_gather | solution.py:34
  222.7 154.9 %copy-start.1 = (f32[256,128]{1,0:T(8,128)S(1)}, f32[256,128]{1,0:T(8,128)}, u32[]{:S(2)}) copy-start(f32[256,128]{1,0:T(8,128)} %param.6) | copy-start | bytes 393220
  222.7 201.1 %all-to-all-start = ((bf16[16,256,256]{1,2,0:T(8,128)(2,1)}), bf16[16,256,256]{1,2,0:T(8,128)(2,1)}, u32[]{:S(2)}, u32[]{:S(2)}) async-start(bf16[16,256,256]{1,2,0:T(8,128)(2,1)} %copy.6), calls=%async_computation | async-start | bytes 4194304 | tf_op jit(solution)/shard_map/all_to_all | solution.py:33
  249.1 174.7 %copy-start.2 = (f32[256,128]{1,0:T(8,128)S(1)}, f32[256,128]{1,0:T(8,128)}, u32[]{:S(2)}) copy-start(f32[256,128]{1,0:T(8,128)} %param.7) | copy-start | bytes 393220
Sparse Core Ops, SparseCore 0:
  219.6 157.8 all-reduce.2
  380.4 43.3 all-gather.1
where the time goes:
time: 434 us
  blocking collectives  202 us (47%)
  waiting for transfers between devices  172 us (40%)
  starting transfers between devices  26.5 us (6%)
  between operations  14.1 us (3%)
  matrix products  13.7 us (3%)
    psum x1, blocking collectives, shards(): summed = lax.psum(contract_first(out_grads, tokens_in), 'dp')  202 us
    psum x1, waiting for transfers between devices, from_root(): return lax.psum(kept, axis)  128 us
    all_gather x1, waiting for transfers between devices, shards(): lax.all_gather(own_tile, 'node', axis=1, tiled=True)  43.6 us
    all_to_all x1, starting transfers between devices, shards(): lax.all_to_all(row_panel, 'node', split_axis=0, concat_axis=1, tiled=True)  26.5 us
    dot_general x2, matrix products, contract_first(): lax.dot_general(left, right, (((0,), (0,)), ((), ())), preferred_element_...  10.4 us
  transfers between devices with their start and end apart: 3, of which 2 were waited for; matrix products, arithmetic and copies ran while one was open for 1% of the time, Pallas kernels for 0%

commit v1 on v0

v1 whole, which is shorter than its diff:
```python
import jax
import jax.numpy as jnp
from jax import lax
from jax.experimental import pallas as pl
from jax.experimental.pallas import tpu as pltpu
from jax.sharding import PartitionSpec as P

MESH = pl.DeviceIdType.MESH
F32, BF16 = jnp.float32, jnp.bfloat16
decay = 0.95
NZ, NX, NODE = 16, 4, 16
TOK, BAND, WIDE, HALF, SUB = 1024, 256, 256, 128, 64


def dot(a, b):
    return lax.dot_general(a, b, (((1,), (0,)), ((), ())), preferred_element_type=F32)


def dot_t(a, b):
    return lax.dot_general(a, b, (((1,), (1,)), ((), ())), preferred_element_type=F32)


def group(g):
    return [0] if g == 0 else [8] if g == 8 else [g, NZ - g]


def kernel(
    tok, og, lold, rold, lout, rout,
    tokt, ogv, keep, ysend, yrecv, zsend, zrecv, ga, sib, at, rsend, rrecv, xt, bz, lacc, lrecv,
    og_sem, y_s, y_r, z_s, z_r, a_s, a_r, c_s, c_r, r_s, r_r, x_s, x_r, lz_s, lz_r, ly_s, lc_s, b_r, f_s, f_r,
):
    dp, node = lax.axis_index("dp"), lax.axis_index("node")
    z, yh = dp // 2, dp % 2
    yl, x, core = node // 8, (node // 2) % 4, node % 2
    y = yh * 2 + yl
    chip = yh * 8 + node // 2

    def at_z(k):
        return {"dp": ((z + k + NZ) % NZ) * 2 + yh, "node": node}

    def at_x(k):
        return {"dp": dp, "node": yl * 8 + ((x + k) % NX) * 2 + core}

    def at_y(k):
        yy = (y + k) % 4
        return {"dp": z * 2 + yy // 2, "node": (yy % 2) * 8 + x * 2 + core}

    partner = {"dp": z * 2 + 1 - yh, "node": node}
    sibling = {"dp": dp, "node": node + 1 - 2 * core}
    up, down = at_z(1), at_z(-1)

    def send(src, dst, ss, rs, to):
        return pltpu.make_async_remote_copy(
            src_ref=src, dst_ref=dst, send_sem=ss, recv_sem=rs, device_id=to, device_id_type=MESH
        )

    def og_copy(n):
        m = (n + 1) // 2
        t = 8 - m
        d = (z + jnp.where(n % 2 == 1, t, NZ - t)) % NZ
        return pltpu.make_async_copy(
            og.at[:, pl.ds(pl.multiple_of(d * WIDE, WIDE), WIDE)], ogv.at[n], og_sem.at[n]
        )

    barrier = pltpu.get_barrier_semaphore()
    for to in (up, down):
        pl.semaphore_signal(barrier, inc=1, device_id=to, device_id_type=MESH)

    def greet(k, carry):
        other = (node + k) % NODE
        pl.semaphore_signal(barrier, inc=1, device_id={"dp": z * 2 + 1 - yh, "node": other}, device_id_type=MESH)

        @pl.when(k > 0)
        def _():
            pl.semaphore_signal(barrier, inc=1, device_id={"dp": dp, "node": other}, device_id_type=MESH)

        return carry

    lax.fori_loop(0, NODE, greet, 0)

    def og_start(n, carry):
        og_copy(n).start()
        return carry

    lax.fori_loop(0, NZ, og_start, 0)

    for c in range(4):
        tokt[:, c * 256 : (c + 1) * 256] = tok[c * 256 : (c + 1) * 256, :].T
    pl.semaphore_wait(barrier, 2 + 31)

    def y_copy(n):
        return send(ysend.at[n], yrecv.at[n], y_s.at[n], y_r.at[n], partner)

    mine = pl.multiple_of(yh * HALF, HALF)
    theirs = pl.multiple_of((1 - yh) * HALF, HALF)

    def partial(n, carry):
        og_copy(n).wait()
        block = ogv.at[n]
        ysend[n] = dot(tokt[pl.ds(theirs, HALF), :], block[...]).astype(BF16)
        y_copy(n).start()
        keep[n] = dot(tokt[pl.ds(mine, HALF), :], block[...])
        return carry

    def z_copy(d, t, s):
        rows = pl.ds(s * SUB, SUB)
        return send(
            zsend.at[d, t - 1, rows], zrecv.at[d, t - 1, rows], z_s.at[d, t - 1, s], z_r.at[d, t - 1, s],
            up if d == 0 else down,
        )

    def z_has(d, t, s):
        return t < 8 or s == d

    def z_stage(t):
        for s in range(2):
            for d in range(2):
                if not z_has(d, t, s):
                    continue
                n = 0 if t == 8 else 2 * (8 - t) - 1 + d
                if t == 8 and d == 0 or t < 8 and s == 0:
                    y_copy(n).wait_recv()
                rows = pl.ds(s * SUB, SUB)
                value = keep[n, rows, :] + yrecv[n, rows, :].astype(F32)
                if t < 8 and z_has(d, t + 1, s):
                    z_copy(d, t + 1, s).wait_recv()
                    value = value + zrecv[d, t, rows, :]
                zsend[d, t - 1, rows, :] = value
                z_copy(d, t, s).start()

    def z_wait_send(t):
        for s in range(2):
            for d in range(2):
                if z_has(d, t, s):
                    z_copy(d, t, s).wait_send()

    lax.fori_loop(0, 9, partial, 0)
    z_stage(8)
    lax.fori_loop(9, 11, partial, 0)
    z_stage(7)
    lax.fori_loop(11, 13, partial, 0)
    z_stage(6)
    lax.fori_loop(13, 16, partial, 0)
    for t in range(5, 0, -1):
        z_stage(t)
    y_copy(15).wait_recv()
    for s in range(2):
        rows = pl.ds(s * SUB, SUB)
        value = keep[15, rows, :] + yrecv[15, rows, :].astype(F32)
        for d in range(2):
            z_copy(d, 1, s).wait_recv()
            value = value + zrecv[d, 0, rows, :]
        ga[0, rows, :] = value.astype(BF16)

    def a_has(d, k, s):
        return k < 8 or s == d

    def a_copy(d, k, s):
        rows = pl.ds(s * SUB, SUB)
        src, dst = ((NZ - k + 1) % NZ, NZ - k) if d == 0 else (k - 1, k)
        return send(
            ga.at[src, rows], ga.at[dst, rows], a_s.at[d, k - 1, s], a_r.at[d, k - 1, s], up if d == 0 else down
        )

    def c_copy(r):
        return send(ga.at[r], sib.at[r], c_s.at[r], c_r.at[r], sibling)

    def a_start(k):
        for s in range(2):
            for d in range(2):
                if k > 1 and a_has(d, k - 1, s):
                    a_copy(d, k - 1, s).wait_recv()
                if k < 9 and a_has(d, k, s):
                    a_copy(d, k, s).start()

    on_core = core == z % 2
    on_row = on_core & (yl == z // 8)

    def x_copy(k):
        slot = (NX - k) % NX
        return send(ga.at[0], xt.at[slot], x_s.at[k - 1], x_r.at[slot], at_x(k))

    def lz_plane(k):
        return yl * 8 + ((x + k) % NX) * 2 + core

    def lz_copy(k):
        plane = lz_plane(k)
        slot = (z - plane + NZ) % NZ
        return send(
            ga.at[0] if k == 0 else xt.at[k], bz.at[yh, slot], lz_s.at[k], b_r.at[yh, slot],
            {"dp": plane * 2 + yh, "node": node},
        )

    def bz_here(h, r):
        return send(bz.at[h, r], bz.at[h, r], f_s.at[0], b_r.at[h, r], partner)

    def ly_copy(k, r):
        return send(bz.at[yh, r], bz.at[yh, r], ly_s.at[r, k - 1], b_r.at[yh, r], at_y(k))

    def lc_copy(h, r):
        return send(bz.at[h, r], bz.at[h, r], lc_s.at[h, r], b_r.at[h, r], sibling)

    def left_z():
        for k in range(1, NX):
            x_copy((NX - k) % NX).wait_recv()
        for k in range(NX):
            away = lz_plane(k) != z

            @pl.when(away)
            def _():
                lz_copy(k).start()

            @pl.when(jnp.logical_not(away))
            def _():
                bz[yh, 0] = ga[0] if k == 0 else xt[k]

    def left_y(r):
        @pl.when(on_row)
        def _():
            if r != 0:
                bz_here(yh, r).wait_recv()
            for k in (1, 3, 2):
                ly_copy(k, r).start()

    def left_c(r):
        @pl.when(on_core)
        def _():
            for h in range(2):
                @pl.when(jnp.logical_not(on_row & (yh == h)))
                def _():
                    bz_here(h, r).wait_recv()

                lc_copy(h, r).start()

    def left_dot(r):
        @pl.when(jnp.logical_not(on_core))
        def _():
            for h in range(2):
                bz_here(h, r).wait_recv()

        for h in range(2):
            value = dot_t(ga[r], bz[h, r])
            lacc[h] = value if r == 0 else lacc[h] + value

    def r_copy(r):
        return send(
            rsend.at[r], rrecv.at[chip], r_s.at[r], r_r.at[chip], {"dp": z * 2 + core, "node": (z + r) % NZ}
        )

    def r_self(r):
        return (yh == core) & (node == (z + r) % NZ)

    def right_dot(r):
        c_copy(r).wait_recv()
        value = (dot(at[0], ga[r]) + dot(at[1], sib[r])).astype(BF16)

        @pl.when(r_self(r))
        def _():
            rrecv[chip] = value

        @pl.when(jnp.logical_not(r_self(r)))
        def _():
            rsend[r] = value
            r_copy(r).start()

    a_start(1)
    c_copy(0).start()
    for k in range(1, NX):
        x_copy(k).start()
    slab = pl.ds(pl.multiple_of(core * HALF, HALF), HALF)
    at[0] = ga[0, :, slab].astype(F32).T.astype(BF16)
    for t in range(8, 4, -1):
        z_wait_send(t)
    c_copy(0).wait_recv()
    at[1] = sib[0, :, slab].astype(F32).T.astype(BF16)

    y_groups = {2: [0], 3: [1, 2], 4: [3, 4], 5: [5, 6], 6: [7, 8]}
    for k in range(2, 10):
        step = k - 1
        a_start(k)
        for r in group(step):
            c_copy(r).start()
        if step == 1:
            left_z()
        if step == 1:
            value = (dot(at[0], ga[0]) + dot(at[1], sib[0])).astype(BF16)

            @pl.when(r_self(0))
            def _():
                rrecv[chip] = value

            @pl.when(jnp.logical_not(r_self(0)))
            def _():
                rsend[0] = value
                r_copy(0).start()
        else:
            for r in group(step - 1):
                right_dot(r)
        for g in y_groups.get(step, []):
            for r in group(g):
                left_y(r)
        for g in y_groups.get(step - 1, []):
            for r in group(g):
                left_c(r)
        for g in y_groups.get(step - 2, []):
            for r in group(g):
                left_dot(r)
    right_dot(8)

    def f_copy():
        return send(lacc.at[1 - yh], lrecv, f_s.at[0], f_r.at[0], partner)

    f_copy().start()
    lout[pl.ds(mine, HALF), :] = decay * lold[pl.ds(mine, HALF), :] + (1.0 - decay) * lacc[yh]

    def r_here(i):
        return send(rrecv.at[i], rrecv.at[i], r_s.at[0], r_r.at[i], partner)

    total = None
    for i in range(NZ):
        @pl.when(jnp.logical_not((core == yh) & (chip == i)))
        def _():
            r_here(i).wait_recv()

        piece = rrecv[i].astype(F32)
        total = piece if total is None else total + piece
    rout[...] = decay * rold[...] + (1.0 - decay) * total.T
    f_copy().wait_recv()
    lout[pl.ds(theirs, HALF), :] = decay * lold[pl.ds(theirs, HALF), :] + (1.0 - decay) * lrecv[...]
    f_copy().wait_send()

    for t in range(4, 0, -1):
        z_wait_send(t)
    for k in range(1, 9):
        for s in range(2):
            for d in range(2):
                if a_has(d, k, s):
                    a_copy(d, k, s).wait_send()
    for k in range(1, NX):
        x_copy(k).wait_send()
    for k in range(NX):
        @pl.when(lz_plane(k) != z)
        def _():
            lz_copy(k).wait_send()

    def drain(n, carry):
        y_copy(n).wait_send()
        return carry

    lax.fori_loop(0, NZ, drain, 0)
    for r in range(NZ):
        c_copy(r).wait_send()

        @pl.when(jnp.logical_not(r_self(r)))
        def _():
            r_copy(r).wait_send()

        @pl.when(on_row)
        def _():
            for k in (1, 3, 2):
                ly_copy(k, r).wait_send()

        @pl.when(on_core)
        def _():
            for h in range(2):
                lc_copy(h, r).wait_send()


def shards(tokens_in, out_grads, left_old, right_old):
    dma = pltpu.SemaphoreType.DMA
    vmem = pl.BlockSpec(memory_space=pltpu.VMEM)
    return pl.pallas_call(
        kernel,
        out_shape=(jax.ShapeDtypeStruct((BAND, HALF), F32),) * 2,
        in_specs=[vmem, pl.BlockSpec(memory_space=pl.ANY), vmem, vmem],
        out_specs=(vmem, vmem),
        scratch_shapes=[
            pltpu.VMEM((BAND, TOK), BF16),
            pltpu.VMEM((NZ, TOK, WIDE), BF16),
            pltpu.VMEM((NZ, HALF, WIDE), F32),
            pltpu.VMEM((NZ, HALF, WIDE), BF16),
            pltpu.VMEM((NZ, HALF, WIDE), BF16),
            pltpu.VMEM((2, 8, HALF, WIDE), F32),
            pltpu.VMEM((2, 8, HALF, WIDE), F32),
            pltpu.VMEM((NZ, HALF, WIDE), BF16),
            pltpu.VMEM((NZ, HALF, WIDE), BF16),
            pltpu.VMEM((2, HALF, HALF), BF16),
            pltpu.VMEM((NZ, HALF, WIDE), BF16),
            pltpu.VMEM((NZ, HALF, WIDE), BF16),
            pltpu.VMEM((NX, HALF, WIDE), BF16),
            pltpu.VMEM((2, NZ, HALF, WIDE), BF16),
            pltpu.VMEM((2, HALF, HALF), F32),
            pltpu.VMEM((HALF, HALF), F32),
            dma((NZ,)), dma((NZ,)), dma((NZ,)),
            dma((2, 8, 2)), dma((2, 8, 2)),
            dma((2, 8, 2)), dma((2, 8, 2)),
            dma((NZ,)), dma((NZ,)),
            dma((NZ,)), dma((NZ,)),
            dma((3,)), dma((4,)),
            dma((4,)), dma((1,)),
            dma((NZ, 3)), dma((2, NZ)), dma((2, NZ)),
            dma((1,)), dma((1,)),
        ],
        compiler_params=pltpu.CompilerParams(
            collective_id=0, has_side_effects=True, vmem_limit_bytes=48 * 2**20
        ),
        cost_estimate=pl.CostEstimate(flops=2 * TOK * BAND * 4096, bytes_accessed=TOK * 4096 * 2, transcendentals=0),
    )(tokens_in, out_grads, left_old, right_old)


def solution(mesh):
    return jax.shard_map(
        shards,
        mesh=mesh,
        in_specs=(P("dp", "node"), P("dp", None), P("node", "dp"), P("node", "dp")),
        out_specs=(P("node", "dp"), P("node", "dp")),
        check_vma=False,
    )
```

time: 434 us -> 135 us (0.31)
  the two profiles are of different devices: /device:TPU:1 before, /device:TPU:8 now
where the time goes in v1:
time: 135 us
  Pallas kernels  130 us (96%)
  local copies, waits for them, and re-layouts  4.15 us (3%)
    pallas_call x1, Pallas kernels, shards(): pl.pallas_call(kernel, out_shape=(jax.ShapeDtypeStruct((BAND, HALF), F32)...  130 us
    unnamed x8, local copies, waits for them, and re-layouts  4.15 us

profile of v1, /device:TPU:8, one launch (start us, length us, event | category | flops | bytes accessed | tf_op | source)
XLA Modules:
  0.0 135.0 jit_solution(13154851343501504832)
XLA Ops:
  0.6 0.0 copy-start
  0.6 1.0 copy-done
  1.7 0.0 copy-start.1
  1.7 0.9 copy-done.1
  2.6 0.0 copy-start.2
  2.6 0.9 copy-done.2
  3.5 130.2 %shard_map.59 = (f32[256,128]{1,0:T(8,128)S(1)}, f32[256,128]{1,0:T(8,128)S(1)}) custom-call(bf16[1024,256]{1,0:T(8,128)(2,1)S(1)} %copy-done, bf16[1024,4096]{1,0:T(8,128)(2,1)} %og.1, f32[256,128]{1,0:T(8,128)S(1)} %copy-done.1, f32[256,128]{1,0:T(8,128)S(1)} %copy-done.2), custom_call_target="tpu_custom_call" | custom-call | flops 2147483648 | bytes 8388608 | tf_op jit(solution)/shard_map/pallas_call | solution.py:372
  133.7 0.7 copy.8
  134.4 0.7 copy.9
Async XLA Ops:
  0.6 1.0 copy-start
  1.7 0.9 copy-start.1
  2.6 0.9 copy-start.2

commit v2 on v1

v2 whole, which is shorter than its diff:
```python
import jax
import jax.numpy as jnp
from jax import lax
from jax.experimental import pallas as pl
from jax.experimental.pallas import tpu as pltpu
from jax.sharding import PartitionSpec as P

MESH = pl.DeviceIdType.MESH
F32, BF16 = jnp.float32, jnp.bfloat16
decay = 0.95
NZ, NODE = 16, 16
TOK, BAND, WIDE, HALF, SUB = 1024, 256, 256, 128, 64
PARTS = 4
PART = HALF // PARTS


def dot(a, b):
    return lax.dot_general(a, b, (((1,), (0,)), ((), ())), preferred_element_type=F32)


def dot_t(a, b):
    return lax.dot_general(a, b, (((1,), (1,)), ((), ())), preferred_element_type=F32)


def group(g):
    return [0] if g == 0 else [8] if g == 8 else [g, NZ - g]


def kernel(
    tok_in, og, lold_in, rold_in, lout, rout,
    tok, lold, rold, tokt, ogv, keep, ysend, yrecv, zsend, zrecv, ga, at, rsend, rrecv, bz, lacc, lrecv,
    in_sem, og_sem, y_s, y_r, z_s, z_r, a_s, a_r, c_s, c_r, r_s, r_r, t_s, b_s, b_r, f_s, f_r,
):
    dp, node = lax.axis_index("dp"), lax.axis_index("node")
    z, yh = dp // 2, dp % 2
    core = node % 2
    chip = yh * 8 + node // 2

    def at_z(k):
        return {"dp": ((z + k + NZ) % NZ) * 2 + yh, "node": node}

    partner = {"dp": z * 2 + 1 - yh, "node": node}
    sibling = {"dp": dp, "node": node + 1 - 2 * core}
    up, down = at_z(1), at_z(-1)

    def send(src, dst, ss, rs, to):
        return pltpu.make_async_remote_copy(
            src_ref=src, dst_ref=dst, send_sem=ss, recv_sem=rs, device_id=to, device_id_type=MESH
        )

    def og_copy(n):
        m = (n + 1) // 2
        t = 8 - m
        d = (z + jnp.where(n % 2 == 1, t, NZ - t)) % NZ
        return pltpu.make_async_copy(
            og.at[:, pl.ds(pl.multiple_of(d * WIDE, WIDE), WIDE)], ogv.at[n], og_sem.at[n]
        )

    def og_start(n, carry):
        og_copy(n).start()
        return carry

    ins = [
        pltpu.make_async_copy(src, dst, in_sem.at[i])
        for i, (src, dst) in enumerate(((tok_in, tok), (lold_in, lold), (rold_in, rold)))
    ]
    ins[0].start()
    barrier = pltpu.get_barrier_semaphore()
    for to in (up, down):
        pl.semaphore_signal(barrier, inc=1, device_id=to, device_id_type=MESH)

    def greet(k, carry):
        other = (node + k) % NODE
        pl.semaphore_signal(barrier, inc=1, device_id={"dp": z * 2 + 1 - yh, "node": other}, device_id_type=MESH)

        @pl.when(k > 0)
        def _():
            pl.semaphore_signal(barrier, inc=1, device_id={"dp": dp, "node": other}, device_id_type=MESH)

        return carry

    lax.fori_loop(0, NODE, greet, 0)
    moves = jnp.logical_not((node == z) & (chip == z) & (core == yh))

    @pl.when(moves)
    def _():
        pl.semaphore_signal(
            barrier, inc=1, device_id={"dp": chip * 2 + core, "node": z}, device_id_type=MESH
        )

    lax.fori_loop(0, NZ, og_start, 0)
    ins[1].start()
    ins[2].start()
    ins[0].wait()
    for c in range(4):
        tokt[:, c * 256 : (c + 1) * 256] = tok[c * 256 : (c + 1) * 256, :].T
    pl.semaphore_wait(barrier, jnp.where(moves, 34, 33))

    def y_copy(n):
        return send(ysend.at[n], yrecv.at[n], y_s.at[n], y_r.at[n], partner)

    mine = pl.multiple_of(yh * HALF, HALF)
    theirs = pl.multiple_of((1 - yh) * HALF, HALF)

    def partial(n, carry):
        og_copy(n).wait()
        block = ogv.at[n]
        ysend[n] = dot(tokt[pl.ds(theirs, HALF), :], block[...]).astype(BF16)
        y_copy(n).start()
        keep[n] = dot(tokt[pl.ds(mine, HALF), :], block[...])
        return carry

    def z_copy(d, t, s):
        rows = pl.ds(s * PART, PART)
        return send(
            zsend.at[d, t - 1, rows], zrecv.at[d, t - 1, rows], z_s.at[d, t - 1, s], z_r.at[d, t - 1, s],
            up if d == 0 else down,
        )

    def z_has(d, t, s):
        return t < 8 or s // (PARTS // 2) == d

    def z_stage(t):
        for s in range(PARTS):
            for d in range(2):
                if not z_has(d, t, s):
                    continue
                n = 0 if t == 8 else 2 * (8 - t) - 1 + d
                if s == 0:
                    y_copy(n).wait_recv()
                rows = pl.ds(s * PART, PART)
                value = keep[n, rows, :] + yrecv[n, rows, :].astype(F32)
                if t < 8 and z_has(d, t + 1, s):
                    z_copy(d, t + 1, s).wait_recv()
                    value = value + zrecv[d, t, rows, :]
                zsend[d, t - 1, rows, :] = value
                z_copy(d, t, s).start()

    def z_wait_send(t):
        for s in range(PARTS):
            for d in range(2):
                if z_has(d, t, s):
                    z_copy(d, t, s).wait_send()

    lax.fori_loop(0, 7, partial, 0)
    z_stage(8)
    lax.fori_loop(7, 10, partial, 0)
    z_stage(7)
    lax.fori_loop(10, 13, partial, 0)
    z_stage(6)
    lax.fori_loop(13, 16, partial, 0)
    for t in range(5, 0, -1):
        z_stage(t)
    y_copy(15).wait_recv()
    for s in range(PARTS):
        rows = pl.ds(s * PART, PART)
        value = keep[15, rows, :] + yrecv[15, rows, :].astype(F32)
        for d in range(2):
            z_copy(d, 1, s).wait_recv()
            value = value + zrecv[d, 0, rows, :]
        ga[0, rows, :] = value.astype(BF16)

    def a_has(d, k, s):
        return k < 8 or s == d

    def a_copy(d, k, s):
        rows = pl.ds(s * SUB, SUB)
        src, dst = ((NZ - k + 1) % NZ, NZ - k) if d == 0 else (k - 1, k)
        return send(
            ga.at[src, rows], ga.at[dst, rows], a_s.at[d, k - 1, s], a_r.at[d, k - 1, s], up if d == 0 else down
        )

    def c_copy(r):
        return send(ga.at[r, pl.ds(0, HALF)], ga.at[r, pl.ds(HALF, HALF)], c_s.at[r], c_r.at[r], sibling)

    def a_start(k):
        for s in range(2):
            for d in range(2):
                if k > 1 and a_has(d, k - 1, s):
                    a_copy(d, k - 1, s).wait_recv()
                if k < 9 and a_has(d, k, s):
                    a_copy(d, k, s).start()

    own = (chip - z + NZ) % NZ
    stays = (node == z) & (chip == z) & (core == yh)

    def t_copy():
        return send(
            ga.at[0, pl.ds(0, HALF)], bz.at[(z - node + NZ) % NZ], t_s.at[0], b_r.at[(z - node + NZ) % NZ],
            {"dp": node * 2 + z // 8, "node": (z % 8) * 2 + yh},
        )

    def b_here(r):
        return send(bz.at[r], bz.at[r], t_s.at[0], b_r.at[r], partner)

    def b_copy(k):
        to = (chip + k) % NZ
        return send(
            bz.at[own], bz.at[own], b_s.at[k - 1], b_r.at[own], {"dp": z * 2 + to // 8, "node": (to % 8) * 2 + core}
        )

    def left_spread(low, high):
        far = jnp.minimum(own, NZ - own)

        @pl.when((far >= low) & (far <= high))
        def _():
            @pl.when(jnp.logical_not(stays))
            def _():
                b_here(own).wait_recv()

            def go(k, carry):
                b_copy(k).start()
                return carry

            lax.fori_loop(1, NZ, go, 0)

    def left_dot(groups):
        tiles = [r for g in groups for r in group(g)]
        for r in tiles:
            @pl.when(own != r)
            def _():
                b_here(r).wait_recv()

        value = lacc[...] if tiles[0] != 0 else None
        for r in tiles:
            term = dot_t(ga[r], bz[r])
            value = term if value is None else value + term
        lacc[...] = value

    def r_copy(r):
        return send(
            rsend.at[r], rrecv.at[chip], r_s.at[r], r_r.at[chip], {"dp": z * 2 + core, "node": (z + r) % NZ}
        )

    def r_self(r):
        return (yh == core) & (node == (z + r) % NZ)

    def right_dot(r):
        value = dot(at[...], ga[r]).astype(BF16)

        @pl.when(r_self(r))
        def _():
            rrecv[chip] = value

        @pl.when(jnp.logical_not(r_self(r)))
        def _():
            rsend[r] = value
            r_copy(r).start()

    a_start(1)
    c_copy(0).start()

    @pl.when(stays)
    def _():
        bz[0] = ga[0, :HALF, :]

    @pl.when(jnp.logical_not(stays))
    def _():
        t_copy().start()

    slab = pl.ds(pl.multiple_of(core * HALF, HALF), HALF)
    c_copy(0).wait_recv()
    at[...] = ga[0, :, slab].astype(F32).T.astype(BF16)
    def drain(n, carry):
        y_copy(n).wait_send()
        return carry

    right_at = {5: (0, 1, 2), 6: (3, 4, 5), 7: (6, 7), 8: (8,)}
    for step in range(1, 9):
        a_start(step + 1)
        for r in group(step):
            c_copy(r).start()
        if step == 1:
            z_wait_send(8)
            z_wait_send(7)
            lax.fori_loop(0, NZ, drain, 0)
        if step == 2:
            left_spread(0, 2)
        if step == 3:
            left_spread(3, 5)
        if step == 4:
            left_spread(6, 8)
        for r in group(step):
            c_copy(r).wait_recv()
        for g in right_at.get(step, ()):
            for r in group(g):
                right_dot(r)
        if step == 7:
            left_dot((0, 1, 2))
        if step in (1, 2, 3):
            z_wait_send(8 - 2 * step)
            z_wait_send(7 - 2 * step)
    left_dot((3, 4, 5))
    left_dot((6, 7, 8))

    ins[1].wait()
    ins[2].wait()

    def f_copy(j):
        return send(
            lacc.at[pl.ds(j * HALF, HALF)], lrecv.at[yh], f_s.at[j], f_r.at[yh],
            {"dp": z * 2 + core, "node": node if j == 0 else node + 1 - 2 * core},
        )

    def f_here(h):
        return send(lrecv.at[h], lrecv.at[h], f_s.at[0], f_r.at[h], partner)

    f_copy(1).start()

    @pl.when(yh == core)
    def _():
        lrecv[yh] = lacc[:HALF, :]

    @pl.when(yh != core)
    def _():
        f_copy(0).start()

    def r_here(i):
        return send(rrecv.at[i], rrecv.at[i], r_s.at[0], r_r.at[i], partner)

    total = None
    for i in range(NZ):
        @pl.when(jnp.logical_not((core == yh) & (chip == i)))
        def _():
            r_here(i).wait_recv()

        piece = rrecv[i].astype(F32)
        total = piece if total is None else total + piece
    rout[...] = decay * rold[...] + (1.0 - decay) * total.T
    for h in range(2):
        @pl.when(jnp.logical_not((core == yh) & (yh == h)))
        def _():
            f_here(h).wait_recv()

        rows = slice(h * HALF, (h + 1) * HALF)
        lout[rows, :] = decay * lold[rows, :] + (1.0 - decay) * lrecv[h]

    f_copy(1).wait_send()

    @pl.when(yh != core)
    def _():
        f_copy(0).wait_send()

    for k in range(1, 9):
        for s in range(2):
            for d in range(2):
                if a_has(d, k, s):
                    a_copy(d, k, s).wait_send()

    @pl.when(jnp.logical_not(stays))
    def _():
        t_copy().wait_send()

    def b_drain(k, carry):
        b_copy(k).wait_send()
        return carry

    lax.fori_loop(1, NZ, b_drain, 0)
    for r in range(NZ):
        c_copy(r).wait_send()

        @pl.when(jnp.logical_not(r_self(r)))
        def _():
            r_copy(r).wait_send()


def shards(tokens_in, out_grads, left_old, right_old):
    dma = pltpu.SemaphoreType.DMA
    vmem = pl.BlockSpec(memory_space=pltpu.VMEM)
    return pl.pallas_call(
        kernel,
        out_shape=(jax.ShapeDtypeStruct((BAND, HALF), F32),) * 2,
        in_specs=[pl.BlockSpec(memory_space=pl.ANY)] * 4,
        out_specs=(vmem, vmem),
        scratch_shapes=[
            pltpu.VMEM((TOK, BAND), BF16),
            pltpu.VMEM((BAND, HALF), F32),
            pltpu.VMEM((BAND, HALF), F32),
            pltpu.VMEM((BAND, TOK), BF16),
            pltpu.VMEM((NZ, TOK, WIDE), BF16),
            pltpu.VMEM((NZ, HALF, WIDE), F32),
            pltpu.VMEM((NZ, HALF, WIDE), BF16),
            pltpu.VMEM((NZ, HALF, WIDE), BF16),
            pltpu.VMEM((2, 8, HALF, WIDE), F32),
            pltpu.VMEM((2, 8, HALF, WIDE), F32),
            pltpu.VMEM((NZ, BAND, WIDE), BF16),
            pltpu.VMEM((HALF, BAND), BF16),
            pltpu.VMEM((NZ, HALF, WIDE), BF16),
            pltpu.VMEM((NZ, HALF, WIDE), BF16),
            pltpu.VMEM((NZ, HALF, WIDE), BF16),
            pltpu.VMEM((BAND, HALF), F32),
            pltpu.VMEM((2, HALF, HALF), F32),
            dma((3,)), dma((NZ,)), dma((NZ,)), dma((NZ,)),
            dma((2, 8, PARTS)), dma((2, 8, PARTS)),
            dma((2, 8, 2)), dma((2, 8, 2)),
            dma((NZ,)), dma((NZ,)),
            dma((NZ,)), dma((NZ,)),
            dma((1,)), dma((NZ - 1,)), dma((NZ,)),
            dma((2,)), dma((2,)),
        ],
        compiler_params=pltpu.CompilerParams(
            collective_id=0, has_side_effects=True, vmem_limit_bytes=60 * 2**20
        ),
        cost_estimate=pl.CostEstimate(flops=2 * TOK * BAND * 4096, bytes_accessed=TOK * 4096 * 2, transcendentals=0),
    )(tokens_in, out_grads, left_old, right_old)


def solution(mesh):
    return jax.shard_map(
        shards,
        mesh=mesh,
        in_specs=(P("dp", "node"), P("dp", None), P("node", "dp"), P("node", "dp")),
        out_specs=(P("node", "dp"), P("node", "dp")),
        check_vma=False,
    )
```

time: 135 us -> 102 us (0.76)
  the two profiles are of different devices: /device:TPU:8 before, /device:TPU:1 now
where the time goes in v2:
time: 102 us; the launch traced here: 101 us
  Pallas kernels  97.2 us (95%)
  local copies, waits for them, and re-layouts  3.14 us (3%)
    pallas_call x1, Pallas kernels, shards(): pl.pallas_call(kernel, out_shape=(jax.ShapeDtypeStruct((BAND, HALF), F32)...  97.2 us
    unnamed x2, local copies, waits for them, and re-layouts  3.14 us

profile of v2, /device:TPU:1, one launch (start us, length us, event | category | flops | bytes accessed | tf_op | source)
XLA Modules:
  0.0 101.0 jit_solution(755830212939166172)
XLA Ops:
  0.6 97.2 %shard_map.59 = (f32[256,128]{1,0:T(8,128)}, f32[256,128]{1,0:T(8,128)}) custom-call(bf16[1024,256]{1,0:T(8,128)(2,1)} %tok_in.1, bf16[1024,4096]{1,0:T(8,128)(2,1)} %og.1, f32[256,128]{1,0:T(8,128)} %lold_in.1, f32[256,128]{1,0:T(8,128)} %rold_in.1), custom_call_target="tpu_custom_call" | custom-call | flops 2147483648 | bytes 8388608 | tf_op jit(solution)/shard_map/pallas_call | solution.py:370
  97.9 1.6 %copy.8 = f32[256,128]{1,0:T(8,128)} copy(f32[256,128]{1,0:T(8,128)} %get-tuple-element.4) | data formatting | bytes 262144
  99.4 1.6 %copy.9 = f32[256,128]{1,0:T(8,128)} copy(f32[256,128]{1,0:T(8,128)} %get-tuple-element.5) | data formatting | bytes 262144

commit v3 on v2

--- a/solution.py
+++ b/solution.py
@@ -27,8 +27,8 @@
 
 
 def kernel(
-    tok_in, og, lold_in, rold_in, lout, rout,
-    tok, lold, rold, tokt, ogv, keep, ysend, yrecv, zsend, zrecv, ga, at, rsend, rrecv, bz, lacc, lrecv,
+    tok_in, og, lout, rout,
+    tok, tokt, ogv, keep, ysend, yrecv, zsend, zrecv, ga, at, rsend, rrecv, bz, lacc, lrecv,
     in_sem, og_sem, y_s, y_r, z_s, z_r, a_s, a_r, c_s, c_r, r_s, r_r, t_s, b_s, b_r, f_s, f_r,
 ):
     dp, node = lax.axis_index("dp"), lax.axis_index("node")
@@ -60,11 +60,10 @@
         og_copy(n).start()
         return carry
 
-    ins = [
-        pltpu.make_async_copy(src, dst, in_sem.at[i])
-        for i, (src, dst) in enumerate(((tok_in, tok), (lold_in, lold), (rold_in, rold)))
-    ]
-    ins[0].start()
+    tok_copy = pltpu.make_async_copy(tok_in, tok, in_sem.at[0])
+    tok_copy.start()
+    for n in range(3):
+        og_copy(n).start()
     barrier = pltpu.get_barrier_semaphore()
     for to in (up, down):
         pl.semaphore_signal(barrier, inc=1, device_id=to, device_id_type=MESH)
@@ -88,10 +87,8 @@
             barrier, inc=1, device_id={"dp": chip * 2 + core, "node": z}, device_id_type=MESH
         )
 
-    lax.fori_loop(0, NZ, og_start, 0)
-    ins[1].start()
-    ins[2].start()
-    ins[0].wait()
+    lax.fori_loop(3, NZ, og_start, 0)
+    tok_copy.wait()
     for c in range(4):
         tokt[:, c * 256 : (c + 1) * 256] = tok[c * 256 : (c + 1) * 256, :].T
     pl.semaphore_wait(barrier, jnp.where(moves, 34, 33))
@@ -293,9 +290,6 @@
     left_dot((3, 4, 5))
     left_dot((6, 7, 8))
 
-    ins[1].wait()
-    ins[2].wait()
-
     def f_copy(j):
         return send(
             lacc.at[pl.ds(j * HALF, HALF)], lrecv.at[yh], f_s.at[j], f_r.at[yh],
@@ -314,32 +308,6 @@
     @pl.when(yh != core)
     def _():
         f_copy(0).start()
-
-    def r_here(i):
-        return send(rrecv.at[i], rrecv.at[i], r_s.at[0], r_r.at[i], partner)
-
-    total = None
-    for i in range(NZ):
-        @pl.when(jnp.logical_not((core == yh) & (chip == i)))
-        def _():
-            r_here(i).wait_recv()
-
-        piece = rrecv[i].astype(F32)
-        total = piece if total is None else total + piece
-    rout[...] = decay * rold[...] + (1.0 - decay) * total.T
-    for h in range(2):
-        @pl.when(jnp.logical_not((core == yh) & (yh == h)))
-        def _():
-            f_here(h).wait_recv()
-
-        rows = slice(h * HALF, (h + 1) * HALF)
-        lout[rows, :] = decay * lold[rows, :] + (1.0 - decay) * lrecv[h]
-
-    f_copy(1).wait_send()
-
-    @pl.when(yh != core)
-    def _():
-        f_copy(0).wait_send()
 
     for k in range(1, 9):
         for s in range(2):
@@ -359,6 +327,33 @@
     for r in range(NZ):
         c_copy(r).wait_send()
 
+    def r_here(i):
+        return send(rrecv.at[i], rrecv.at[i], r_s.at[0], r_r.at[i], partner)
+
+    total = None
+    for i in range(NZ):
+        @pl.when(jnp.logical_not((core == yh) & (chip == i)))
+        def _():
+            r_here(i).wait_recv()
+
+        piece = rrecv[i].astype(F32)
+        total = piece if total is None else total + piece
+    rout[...] = total.T
+    for h in range(2):
+        @pl.when(jnp.logical_not((core == yh) & (yh == h)))
+        def _():
+            f_here(h).wait_recv()
+
+        rows = slice(h * HALF, (h + 1) * HALF)
+        lout[rows, :] = lrecv[h]
+
+    f_copy(1).wait_send()
+
+    @pl.when(yh != core)
+    def _():
+        f_copy(0).wait_send()
+
+    for r in range(NZ):
         @pl.when(jnp.logical_not(r_self(r)))
         def _():
             r_copy(r).wait_send()
@@ -367,15 +362,13 @@
 def shards(tokens_in, out_grads, left_old, right_old):
     dma = pltpu.SemaphoreType.DMA
     vmem = pl.BlockSpec(memory_space=pltpu.VMEM)
-    return pl.pallas_call(
+    left_new, right_new = pl.pallas_call(
         kernel,
         out_shape=(jax.ShapeDtypeStruct((BAND, HALF), F32),) * 2,
-        in_specs=[pl.BlockSpec(memory_space=pl.ANY)] * 4,
+        in_specs=[pl.BlockSpec(memory_space=pl.ANY)] * 2,
         out_specs=(vmem, vmem),
         scratch_shapes=[
             pltpu.VMEM((TOK, BAND), BF16),
-            pltpu.VMEM((BAND, HALF), F32),
-            pltpu.VMEM((BAND, HALF), F32),
             pltpu.VMEM((BAND, TOK), BF16),
             pltpu.VMEM((NZ, TOK, WIDE), BF16),
             pltpu.VMEM((NZ, HALF, WIDE), F32),
@@ -390,7 +383,7 @@
             pltpu.VMEM((NZ, HALF, WIDE), BF16),
             pltpu.VMEM((BAND, HALF), F32),
             pltpu.VMEM((2, HALF, HALF), F32),
-            dma((3,)), dma((NZ,)), dma((NZ,)), dma((NZ,)),
+            dma((1,)), dma((NZ,)), dma((NZ,)), dma((NZ,)),
             dma((2, 8, PARTS)), dma((2, 8, PARTS)),
             dma((2, 8, 2)), dma((2, 8, 2)),
             dma((NZ,)), dma((NZ,)),
@@ -402,7 +395,10 @@
             collective_id=0, has_side_effects=True, vmem_limit_bytes=60 * 2**20
         ),
         cost_estimate=pl.CostEstimate(flops=2 * TOK * BAND * 4096, bytes_accessed=TOK * 4096 * 2, transcendentals=0),
-    )(tokens_in, out_grads, left_old, right_old)
+    )(tokens_in, out_grads)
+    left_out = decay * left_old + (1.0 - decay) * left_new
+    right_out = decay * right_old + (1.0 - decay) * right_new
+    return left_out, right_out
 
 
 def solution(mesh):

time: 102 us -> 101 us (level)
  local copies, waits for them, and re-layouts: 3.14 us -> 0.01 us
  other arithmetic: 0 us -> 1.71 us
    unnamed x2 -> x4, local copies, waits for them, and re-layouts: 3.14 us -> 0.01 us
    add x0 -> x1, other arithmetic: none -> 1.71 us  [shards(): right_out = decay * right_old + (1.0 - decay) * right_new]
where the time goes in v3:
time: 101 us; the launch traced here: 99.6 us
  Pallas kernels  97.2 us (96%)
  other arithmetic  1.71 us (2%)
    pallas_call x1, Pallas kernels, shards(): pl.pallas_call(kernel, out_shape=(jax.ShapeDtypeStruct((BAND, HALF), F32)...  97.2 us

profile of v3, /device:TPU:1, one launch (start us, length us, event | category | flops | bytes accessed | tf_op | source)
XLA Modules:
  0.0 99.6 jit_solution(4819669726603933958)
XLA Ops:
  0.6 0.0 copy-start
  0.6 0.0 copy-start.1
  0.7 97.2 %shard_map.59 = (f32[256,128]{1,0:T(8,128)}, f32[256,128]{1,0:T(8,128)}) custom-call(bf16[1024,256]{1,0:T(8,128)(2,1)} %tok_in.1, bf16[1024,4096]{1,0:T(8,128)(2,1)} %og.1), custom_call_target="tpu_custom_call" | custom-call | flops 2147483648 | bytes 8388608 | tf_op jit(solution)/shard_map/pallas_call | solution.py:365
  97.8 0.0 copy-done
  97.8 0.0 copy-done.1
  97.9 1.7 %multiply_add_fusion = (f32[256,128]{1,0:T(8,128)}, f32[256,128]{1,0:T(8,128)}) fusion(f32[256,128]{1,0:T(8,128)} %get-tuple-element.5, f32[256,128]{1,0:T(8,128)S(1)} %copy-done, f32[256,128]{1,0:T(8,128)} %get-tuple-element.4, f32[256,128]{1,0:T(8,128)S(1)} %copy-done.1), kind=kLoop, calls=%fused_computation | loop fusion | flops 196608 | bytes 786432 | tf_op jit(solution)/shard_map/add | solution.py:400
Async XLA Ops:
  0.6 97.2 %copy-start = (f32[256,128]{1,0:T(8,128)S(1)}, f32[256,128]{1,0:T(8,128)}, u32[]{:S(2)}) copy-start(f32[256,128]{1,0:T(8,128)} %param.7) | copy-start | bytes 393220
  0.6 97.2 %copy-start.1 = (f32[256,128]{1,0:T(8,128)S(1)}, f32[256,128]{1,0:T(8,128)}, u32[]{:S(2)}) copy-start(f32[256,128]{1,0:T(8,128)} %param.6) | copy-start | bytes 393220

commit v4 on v3

--- a/solution.py
+++ b/solution.py
@@ -89,22 +89,24 @@
 
     lax.fori_loop(3, NZ, og_start, 0)
     tok_copy.wait()
+    mine = pl.multiple_of(yh * HALF, HALF)
+    theirs = pl.multiple_of((1 - yh) * HALF, HALF)
     for c in range(4):
-        tokt[:, c * 256 : (c + 1) * 256] = tok[c * 256 : (c + 1) * 256, :].T
+        rows = slice(c * 256, (c + 1) * 256)
+        tokt[:HALF, rows] = tok[rows, pl.ds(mine, HALF)].T
+        tokt[HALF:, rows] = tok[rows, pl.ds(theirs, HALF)].T
     pl.semaphore_wait(barrier, jnp.where(moves, 34, 33))
 
     def y_copy(n):
         return send(ysend.at[n], yrecv.at[n], y_s.at[n], y_r.at[n], partner)
 
-    mine = pl.multiple_of(yh * HALF, HALF)
-    theirs = pl.multiple_of((1 - yh) * HALF, HALF)
 
     def partial(n, carry):
         og_copy(n).wait()
-        block = ogv.at[n]
-        ysend[n] = dot(tokt[pl.ds(theirs, HALF), :], block[...]).astype(BF16)
+        block = dot(tokt[...], ogv[n])
+        ysend[n] = block[HALF:, :].astype(BF16)
         y_copy(n).start()
-        keep[n] = dot(tokt[pl.ds(mine, HALF), :], block[...])
+        keep[n] = block[:HALF, :]
         return carry
 
     def z_copy(d, t, s):

time: 101 us -> 100 us (0.990); the launches traced: 99.6 us -> 99.7 us
  no operation moved by 1% of the time
where the time goes in v4:
time: 100 us; the launch traced here: 99.7 us
  Pallas kernels  97.3 us (97%)
  other arithmetic  1.71 us (2%)
    pallas_call x1, Pallas kernels, shards(): pl.pallas_call(kernel, out_shape=(jax.ShapeDtypeStruct((BAND, HALF), F32)...  97.3 us

profile of v4, /device:TPU:1, one launch (start us, length us, event | category | flops | bytes accessed | tf_op | source)
XLA Modules:
  0.0 99.7 jit_solution(5929243471026492015)
XLA Ops:
  0.6 0.0 copy-start
  0.6 0.0 copy-start.1
  0.7 97.3 %shard_map.59 = (f32[256,128]{1,0:T(8,128)}, f32[256,128]{1,0:T(8,128)}) custom-call(bf16[1024,256]{1,0:T(8,128)(2,1)} %tok_in.1, bf16[1024,4096]{1,0:T(8,128)(2,1)} %og.1), custom_call_target="tpu_custom_call" | custom-call | flops 2147483648 | bytes 8388608 | tf_op jit(solution)/shard_map/pallas_call | solution.py:367
  97.9 0.0 copy-done
  97.9 0.0 copy-done.1
  97.9 1.7 %multiply_add_fusion = (f32[256,128]{1,0:T(8,128)}, f32[256,128]{1,0:T(8,128)}) fusion(f32[256,128]{1,0:T(8,128)} %get-tuple-element.5, f32[256,128]{1,0:T(8,128)S(1)} %copy-done, f32[256,128]{1,0:T(8,128)} %get-tuple-element.4, f32[256,128]{1,0:T(8,128)S(1)} %copy-done.1), kind=kLoop, calls=%fused_computation | loop fusion | flops 196608 | bytes 786432 | tf_op jit(solution)/shard_map/add | solution.py:402
Async XLA Ops:
  0.6 97.3 %copy-start = (f32[256,128]{1,0:T(8,128)S(1)}, f32[256,128]{1,0:T(8,128)}, u32[]{:S(2)}) copy-start(f32[256,128]{1,0:T(8,128)} %param.7) | copy-start | bytes 393220
  0.6 97.3 %copy-start.1 = (f32[256,128]{1,0:T(8,128)S(1)}, f32[256,128]{1,0:T(8,128)}, u32[]{:S(2)}) copy-start(f32[256,128]{1,0:T(8,128)} %param.6) | copy-start | bytes 393220

commit v5 on v4

--- a/solution.py
+++ b/solution.py
@@ -246,16 +246,16 @@
             rsend[r] = value
             r_copy(r).start()
 
+    @pl.when(jnp.logical_not(stays))
+    def _():
+        t_copy().start()
+
     a_start(1)
     c_copy(0).start()
 
     @pl.when(stays)
     def _():
         bz[0] = ga[0, :HALF, :]
-
-    @pl.when(jnp.logical_not(stays))
-    def _():
-        t_copy().start()
 
     slab = pl.ds(pl.multiple_of(core * HALF, HALF), HALF)
     c_copy(0).wait_recv()

time: 100 us -> 103 us (1.030)
  Pallas kernels: 97.3 us -> 99.7 us
    pallas_call x1, Pallas kernels: 97.3 us -> 99.7 us  [shards(): pl.pallas_call(kernel, out_shape=(jax.ShapeDtypeStruct((BAND, HALF), F32)...]
where the time goes in v5:
time: 103 us; the launch traced here: 102 us
  Pallas kernels  99.7 us (97%)
  other arithmetic  1.71 us (2%)
    pallas_call x1, Pallas kernels, shards(): pl.pallas_call(kernel, out_shape=(jax.ShapeDtypeStruct((BAND, HALF), F32)...  99.7 us

profile of v5, /device:TPU:1, one launch (start us, length us, event | category | flops | bytes accessed | tf_op | source)
XLA Modules:
  0.0 102.1 jit_solution(11206046812066586293)
XLA Ops:
  0.6 0.0 copy-start
  0.6 0.0 copy-start.1
  0.7 99.7 %shard_map.59 = (f32[256,128]{1,0:T(8,128)}, f32[256,128]{1,0:T(8,128)}) custom-call(bf16[1024,256]{1,0:T(8,128)(2,1)} %tok_in.1, bf16[1024,4096]{1,0:T(8,128)(2,1)} %og.1), custom_call_target="tpu_custom_call" | custom-call | flops 2147483648 | bytes 8388608 | tf_op jit(solution)/shard_map/pallas_call | solution.py:367
  100.3 0.0 copy-done
  100.3 0.0 copy-done.1
  100.4 1.7 %multiply_add_fusion = (f32[256,128]{1,0:T(8,128)}, f32[256,128]{1,0:T(8,128)}) fusion(f32[256,128]{1,0:T(8,128)} %get-tuple-element.5, f32[256,128]{1,0:T(8,128)S(1)} %copy-done, f32[256,128]{1,0:T(8,128)} %get-tuple-element.4, f32[256,128]{1,0:T(8,128)S(1)} %copy-done.1), kind=kLoop, calls=%fused_computation | loop fusion | flops 196608 | bytes 786432 | tf_op jit(solution)/shard_map/add | solution.py:402
Async XLA Ops:
  0.6 99.7 %copy-start = (f32[256,128]{1,0:T(8,128)S(1)}, f32[256,128]{1,0:T(8,128)}, u32[]{:S(2)}) copy-start(f32[256,128]{1,0:T(8,128)} %param.7) | copy-start | bytes 393220
  0.6 99.7 %copy-start.1 = (f32[256,128]{1,0:T(8,128)S(1)}, f32[256,128]{1,0:T(8,128)}, u32[]{:S(2)}) copy-start(f32[256,128]{1,0:T(8,128)} %param.6) | copy-start | bytes 393220
